TPU v7x, 32 devices: a whole 2x2x4 slice. The times are simulated.
32 devices in a mesh: seq: 8 (over z, x), chan: 4 (over y, core).
Axes of the slice: x: 2, y: 2, z: 4, core: 2. Of those that a mesh axis runs over, the one named last changes fastest.
Arguments:
- inner_gate: bfloat16 [4096, 2048], P('seq', 'chan'), may hold values from -6 to 6
- values: bfloat16 [4096, 2048], P('seq', 'chan'), may hold values from -6 to 6
- outer_gate: bfloat16 [4096, 2048], P('seq', 'chan'), may hold values from -6 to 6
- filter_taps: float32 [4096, 2048], P('seq', 'chan'), may hold values from -0.09375 to 0.09375
- skip_gain: float32 [2048], P('chan'), may hold values from -4 to 4
- out_proj: bfloat16 [2048, 2048], P('chan'), may hold values from -0.125 to 0.125
Outputs:
- mixer_out: bfloat16 [4096, 2048], P('seq', 'chan')
All inputs are finite; a program needn't handle non-finite values.
Results may differ from a plain program's by a relative error of at most 0.013.
Values may be sent and summed in bfloat16 or wider, within the bound.
A program may use at most 128 MiB of HBM per device.

v0:
```python
import functools
import math

import jax
import jax.numpy as jnp
import numpy as np
from jax import lax
from jax.experimental import pallas as pl
from jax.experimental.pallas import tpu as pltpu
from jax.sharding import PartitionSpec as P

BLK = 128


def wave_table(length, direction):
    positions = jnp.arange(length, dtype=jnp.int32)
    phases = positions[:, None] * positions[None, :] % length
    angles = phases.astype(jnp.float32) * (2.0 * math.pi / length)
    return (
        jnp.cos(angles).astype(jnp.bfloat16),
        (direction * jnp.sin(angles)).astype(jnp.bfloat16),
    )


def twiddle(row_ids, col_ids, length, direction):
    phases = row_ids * col_ids % length
    angles = phases.astype(jnp.float32) * (2.0 * math.pi / length)
    return (jnp.cos(angles), direction * jnp.sin(angles))


def apply_table(pattern, table, signal):
    table_real, table_imag = table
    signal_real, signal_imag = signal
    out_real = jnp.einsum(pattern, table_real, signal_real, preferred_element_type=jnp.float32)
    out_imag = jnp.einsum(pattern, table_imag, signal_real, preferred_element_type=jnp.float32)
    if signal_imag is not None:
        out_real = out_real - jnp.einsum(
            pattern, table_imag, signal_imag, preferred_element_type=jnp.float32
        )
        out_imag = out_imag + jnp.einsum(
            pattern, table_real, signal_imag, preferred_element_type=jnp.float32
        )
    return (out_real, out_imag)


def twist_round(signal, factor):
    signal_real, signal_imag = signal
    factor_real, factor_imag = factor
    return (
        (signal_real * factor_real - signal_imag * factor_imag).astype(jnp.bfloat16),
        (signal_real * factor_imag + signal_imag * factor_real).astype(jnp.bfloat16),
    )


def lead_forward(signal, lane_table, first, tables, second):
    table_q, table_m = tables
    section = twist_round(apply_table("pk,cpqm->ckqm", lane_table, signal), first)
    shaped = twist_round(apply_table("qj,ckqm->ckjm", table_q, section), second)
    return apply_table("mn,ckjm->ckjn", table_m, shaped)


def lead_inverse(spectrum, tables, second, first):
    table_q, table_m = tables
    shaped = twist_round(apply_table("mn,ckjn->ckjm", table_m, spectrum), second)
    return twist_round(apply_table("qj,ckjm->ckqm", table_q, shaped), first)


def combine(even_part, odd_part, half_cos, half_sin, seq_length):
    return (even_part[0] + (half_cos * odd_part[0] - half_sin * odd_part[1])) / (2.0 * seq_length)


def plain_on_device(inner_gate, values, outer_gate, filter_taps, skip_gain, out_proj):
    seq_count = lax.axis_size("seq")
    my_index = lax.axis_index("seq")
    tokens = inner_gate.shape[0]
    seq_length = tokens * seq_count
    block_count = tokens // BLK
    forward_lane = wave_table(seq_count, -1.0)
    inverse_lane = wave_table(seq_count, 1.0)
    forward_local = (wave_table(block_count, -1.0), wave_table(BLK, -1.0))
    inverse_local = (wave_table(block_count, 1.0), wave_table(BLK, 1.0))
    own_angle = (my_index * tokens + jnp.arange(tokens, dtype=jnp.int32)).astype(
        jnp.float32
    ).reshape(tokens, 1) * (math.pi / seq_length)
    own_cos = jnp.cos(own_angle)
    own_sin = jnp.sin(own_angle)
    mixed = (inner_gate.astype(jnp.float32) * values.astype(jnp.float32)).astype(jnp.bfloat16)
    mixed = lax.optimization_barrier(mixed)
    mixed_wide = mixed.astype(jnp.float32)
    odd_real = (mixed_wide * own_cos).astype(jnp.bfloat16)
    odd_imag = (-(mixed_wide * own_sin)).astype(jnp.bfloat16)
    taps_even = filter_taps.astype(jnp.bfloat16)
    taps_real = (filter_taps * own_cos).astype(jnp.bfloat16)
    taps_imag = (-(filter_taps * own_sin)).astype(jnp.bfloat16)
    spread = (
        lax.all_to_all(mixed, "seq", split_axis=1, concat_axis=0, tiled=True),
        lax.all_to_all(odd_real, "seq", split_axis=1, concat_axis=0, tiled=True),
        lax.all_to_all(odd_imag, "seq", split_axis=1, concat_axis=0, tiled=True),
        lax.all_to_all(taps_even, "seq", split_axis=1, concat_axis=0, tiled=True),
        lax.all_to_all(taps_real, "seq", split_axis=1, concat_axis=0, tiled=True),
        lax.all_to_all(taps_imag, "seq", split_axis=1, concat_axis=0, tiled=True),
    )
    slab_width = spread[0].shape[1]
    slabs = [piece.T.reshape(slab_width, seq_count, block_count, BLK) for piece in spread]
    outer_flat = jnp.arange(block_count, dtype=jnp.int32).reshape(block_count, 1)
    inner_flat = jnp.arange(BLK, dtype=jnp.int32).reshape(1, BLK)
    second_forward = twiddle(outer_flat, inner_flat, tokens, -1.0)
    second_inverse = twiddle(outer_flat, inner_flat, tokens, 1.0)
    lane_index = jnp.arange(seq_count, dtype=jnp.int32).reshape(seq_count, 1, 1)
    row_index = jnp.arange(tokens, dtype=jnp.int32).reshape(1, block_count, BLK)
    first_forward = twiddle(lane_index, row_index, seq_length, -1.0)
    first_inverse = twiddle(lane_index, row_index, seq_length, 1.0)
    signals = ((slabs[0], None), (slabs[1], slabs[2]), (slabs[3], None), (slabs[4], slabs[5]))
    spectra = [
        lead_forward(signal, forward_lane, first_forward, forward_local, second_forward)
        for signal in signals
    ]
    product_even = twist_round(spectra[0], spectra[2])
    product_odd = twist_round(spectra[1], spectra[3])
    back_even = lead_inverse(product_even, inverse_local, second_inverse, first_inverse)
    back_odd = lead_inverse(product_odd, inverse_local, second_inverse, first_inverse)
    even_part = apply_table("pk,ckqm->cpqm", inverse_lane, back_even)
    odd_part = apply_table("pk,ckqm->cpqm", inverse_lane, back_odd)
    lane_angle = (lane_index * tokens + row_index).astype(jnp.float32) * (math.pi / seq_length)
    slab_conv = combine(even_part, odd_part, jnp.cos(lane_angle), jnp.sin(lane_angle), seq_length)
    slab_conv = slab_conv.reshape(slab_width, seq_length).T
    convolved = lax.all_to_all(
        slab_conv.astype(jnp.bfloat16), "seq", split_axis=0, concat_axis=1, tiled=True
    ).astype(slab_conv.dtype)
    gated = (
        outer_gate.astype(jnp.float32)
        * (convolved + skip_gain[None, :] * values.astype(jnp.float32))
    ).astype(jnp.bfloat16)
    partial_value = jnp.dot(gated, out_proj, preferred_element_type=jnp.float32)
    return lax.psum_scatter(
        partial_value.astype(jnp.bfloat16), "chan", scatter_dimension=1, tiled=True
    )


SHIFT = 0.25
MESH = pl.DeviceIdType.MESH


def split_forward(pieces):
    count = len(pieces)
    if count == 1:
        return [(pieces[0], None)]
    even, odd = split_forward(pieces[0::2]), split_forward(pieces[1::2])
    low, high = [], []
    for k in range(count // 2):
        angle = 2.0 * math.pi * (k + SHIFT) / count
        cos, sin = math.cos(angle), math.sin(angle)
        odd_re, odd_im = odd[k]
        even_re, even_im = even[k]
        if odd_im is None:
            turn_re, turn_im = cos * odd_re, -sin * odd_re
            low.append((even_re + turn_re, turn_im))
            high.append((even_re - turn_re, -turn_im))
        else:
            turn_re = cos * odd_re + sin * odd_im
            turn_im = cos * odd_im - sin * odd_re
            low.append((even_re + turn_re, even_im + turn_im))
            high.append((even_re - turn_re, even_im - turn_im))
    return low + high


def split_inverse(bins):
    count = len(bins)
    if count == 1:
        return [bins[0][0]]
    half = count // 2
    even, odd = [], []
    for k in range(half):
        angle = 2.0 * math.pi * (k + SHIFT) / count
        cos, sin = math.cos(angle), math.sin(angle)
        (low_re, low_im), (high_re, high_im) = bins[k], bins[k + half]
        gap_re, gap_im = low_re - high_re, low_im - high_im
        if half == 1:
            even.append((low_re + high_re, None))
            odd.append((cos * gap_re - sin * gap_im, None))
        else:
            even.append((low_re + high_re, low_im + high_im))
            odd.append((cos * gap_re - sin * gap_im, sin * gap_re + cos * gap_im))
    even, odd = split_inverse(even), split_inverse(odd)
    return [piece for pair in zip(even, odd) for piece in pair]


def mixer_kernel(
    lanes,
    groups,
    inner_ref,
    values_ref,
    outer_ref,
    taps_ref,
    skip_ref,
    proj_ref,
    cos_ref,
    sin_ref,
    turn_cos_ref,
    turn_sin_ref,
    out_ref,
    leave,
    arrive,
    sec_re,
    sec_im,
    back_re,
    back_im,
    conv_leave,
    conv_arrive,
    gathered,
    weights,
    total,
    in_send,
    in_recv,
    conv_send,
    conv_recv,
    side_send,
    side_recv,
    proj_send,
    proj_recv,
    proj_own,
):
    me = lax.axis_index("seq")
    slab = lax.axis_index("chan")
    slabs = 4
    tokens = inner_ref.shape[0]
    wide = inner_ref.shape[1] // groups
    each = wide // lanes
    columns = out_ref.shape[1]
    sibling = slab + 1 - 2 * (slab % 2)
    across = (slab + 2) % 4
    corner = (sibling + 2) % 4

    barrier = pltpu.get_barrier_semaphore()

    @pl.loop(1, lanes)
    def _(step):
        pl.semaphore_signal(
            barrier, inc=1, device_id={"seq": (me + step) % lanes}, device_id_type=MESH
        )

    for step in range(1, slabs):
        pl.semaphore_signal(
            barrier, inc=1, device_id={"chan": (slab + step) % slabs}, device_id_type=MESH
        )

    def prepare(g):
        cols = pl.ds(pl.multiple_of(g * wide, wide), wide)
        mixed = inner_ref[:, cols].astype(jnp.float32) * values_ref[:, cols].astype(jnp.float32)
        mixed = mixed.T.astype(jnp.bfloat16)
        taps = taps_ref[:, cols].T.astype(jnp.bfloat16)
        for p in range(lanes):
            leave[g, p, 0] = mixed[p * each : (p + 1) * each, :]
            leave[g, p, 1] = taps[p * each : (p + 1) * each, :]
        arrive[g, me] = leave[g, me]

    def in_copy(g, step, source):
        target = (me + step) % lanes
        return pltpu.make_async_remote_copy(
            src_ref=leave.at[g, target],
            dst_ref=arrive.at[g, source],
            send_sem=in_send.at[g, step],
            recv_sem=in_recv.at[g, step],
            device_id={"seq": target},
            device_id_type=MESH,
        )

    def conv_copy(g, step, source):
        target = (me + step) % lanes
        return pltpu.make_async_remote_copy(
            src_ref=conv_leave.at[g, target],
            dst_ref=conv_arrive.at[g, source],
            send_sem=conv_send.at[g, step],
            recv_sem=conv_recv.at[g, step],
            device_id={"seq": target},
            device_id_type=MESH,
        )

    def proj_copy(step, source):
        target = (slab + step) % slabs
        return pltpu.make_async_remote_copy(
            src_ref=proj_ref.at[:, :, pl.ds(pl.multiple_of(target * columns, columns), columns)],
            dst_ref=weights.at[:, source],
            send_sem=proj_send.at[step],
            recv_sem=proj_recv.at[step],
            device_id={"chan": target},
            device_id_type=MESH,
        )

    def side_copy(g, kind, block, target):
        return pltpu.make_async_remote_copy(
            src_ref=gathered.at[g, block],
            dst_ref=gathered.at[g, block],
            send_sem=side_send.at[g, kind],
            recv_sem=side_recv.at[g, kind],
            device_id={"chan": target},
            device_id_type=MESH,
        )

    prepare(0)
    pl.semaphore_wait(barrier, lanes - 1 + slabs - 1)

    own_proj = pltpu.make_async_copy(
        proj_ref.at[:, :, pl.ds(pl.multiple_of(slab * columns, columns), columns)],
        weights.at[:, slab],
        proj_own,
    )

    @pl.loop(1, lanes)
    def _(step):
        in_copy(0, step, me).start()

    own_proj.start()
    for step in range(1, slabs):
        proj_copy(step, slab).start()

    @pl.loop(1, groups)
    def _(g):
        prepare(g)

        @pl.loop(1, lanes)
        def _(step):
            in_copy(g, step, me).start()

    def dot(left, right):
        return jnp.dot(left, right, preferred_element_type=jnp.float32)

    @pl.loop(0, groups)
    def _(g):
        @pl.loop(1, lanes)
        def _(step):
            in_copy(g, step, (me + lanes - step) % lanes).wait_recv()

        @pl.loop(0, tokens // BLK)
        def _(j):
            span = pl.ds(pl.multiple_of(j * BLK, BLK), BLK)
            for sig in range(2):
                bins = split_forward(
                    [arrive[g, p, sig, :, span].astype(jnp.float32) for p in range(lanes)]
                )
                for k in range(lanes):
                    re, im = bins[k]
                    cos, sin = turn_cos_ref[k : k + 1, span], turn_sin_ref[k : k + 1, span]
                    sec_re[sig, k, :, span] = (re * cos + im * sin).astype(jnp.bfloat16)
                    sec_im[sig, k, :, span] = (im * cos - re * sin).astype(jnp.bfloat16)

        rows = lanes * each
        re = sec_re[...].reshape(2 * rows, tokens)
        im = sec_im[...].reshape(2 * rows, tokens)
        cos, sin = cos_ref[...], sin_ref[...]
        spec_re = dot(re, cos) + dot(im, sin)
        spec_im = dot(im, cos) - dot(re, sin)
        x_re, h_re = spec_re[:rows], spec_re[rows:]
        x_im, h_im = spec_im[:rows], spec_im[rows:]
        prod_re = (x_re * h_re - x_im * h_im).astype(jnp.bfloat16)
        prod_im = (x_re * h_im + x_im * h_re).astype(jnp.bfloat16)
        back_re[...] = (dot(prod_re, cos) - dot(prod_im, sin)).reshape(lanes, each, tokens)
        back_im[...] = (dot(prod_im, cos) + dot(prod_re, sin)).reshape(lanes, each, tokens)

        @pl.loop(0, tokens // BLK)
        def _(j):
            span = pl.ds(pl.multiple_of(j * BLK, BLK), BLK)
            bins = []
            for k in range(lanes):
                re, im = back_re[k, :, span], back_im[k, :, span]
                cos, sin = turn_cos_ref[k : k + 1, span], turn_sin_ref[k : k + 1, span]
                bins.append((re * cos - im * sin, re * sin + im * cos))
            pieces = split_inverse(bins)
            for p in range(lanes):
                conv_leave[g, p, :, span] = (pieces[p] * (1.0 / (lanes * tokens))).astype(
                    jnp.bfloat16
                )

        @pl.loop(1, lanes)
        def _(step):
            conv_copy(g, step, me).start()

        conv_arrive[g, me] = conv_leave[g, me]

    def forward(g):
        side_copy(g, 1, across, across).wait_recv()
        side_copy(g, 2, across, sibling).start()

    for g in range(groups):

        @pl.loop(1, lanes)
        def _(step):
            conv_copy(g, step, (me + lanes - step) % lanes).wait_recv()

        cols = slice(g * wide, (g + 1) * wide)
        conv = conv_arrive[g].astype(jnp.float32).reshape(wide, tokens).T
        gated = outer_ref[:, cols].astype(jnp.float32) * (
            conv + skip_ref[:, cols] * values_ref[:, cols].astype(jnp.float32)
        )
        gathered[g, slab] = gated.astype(jnp.bfloat16)
        side_copy(g, 1, slab, across).start()
        side_copy(g, 0, slab, sibling).start()
        if g > 0:
            forward(g - 1)
    forward(groups - 1)

    own_proj.wait()
    for step in range(1, slabs):
        proj_copy(step, (slab + slabs - step) % slabs).wait_recv()

    for g in range(groups):
        side_copy(g, 0, sibling, sibling).wait_recv()
        side_copy(g, 2, corner, sibling).wait_recv()
        left = jnp.concatenate([gathered[g, j] for j in range(slabs)], axis=1)
        part = dot(left, weights[g].reshape(slabs * wide, columns))
        if g == 0:
            total[...] = part
        elif g < groups - 1:
            total[...] += part
        else:
            out_ref[...] = (total[...] + part).astype(out_ref.dtype)

    @pl.loop(0, groups)
    def _(g):
        @pl.loop(1, lanes)
        def _(step):
            in_copy(g, step, me).wait_send()
            conv_copy(g, step, me).wait_send()

        side_copy(g, 0, slab, sibling).wait_send()
        side_copy(g, 1, slab, across).wait_send()
        side_copy(g, 2, across, sibling).wait_send()

    for step in range(1, slabs):
        proj_copy(step, slab).wait_send()


def kernel_on_device(lanes, groups, inner_gate, values, outer_gate, filter_taps, skip_gain, out_proj):
    slabs = 4
    tokens, channels = inner_gate.shape
    wide = channels // groups
    each = wide // lanes
    columns = out_proj.shape[1] // slabs
    index = np.arange(tokens)
    angles = 2.0 * np.pi * ((index[:, None] * index[None, :]) % tokens) / tokens
    turns = 2.0 * np.pi * (np.arange(lanes)[:, None] + SHIFT) * index[None, :] / (lanes * tokens)
    tables = (
        jnp.asarray(np.cos(angles), jnp.bfloat16),
        jnp.asarray(np.sin(angles), jnp.bfloat16),
        jnp.asarray(np.cos(turns), jnp.float32),
        jnp.asarray(np.sin(turns), jnp.float32),
    )
    here = pl.BlockSpec(memory_space=pltpu.VMEM)
    dma = pltpu.SemaphoreType.DMA
    return pl.pallas_call(
        functools.partial(mixer_kernel, lanes, groups),
        out_shape=jax.ShapeDtypeStruct((tokens, columns), jnp.bfloat16),
        in_specs=[here] * 5 + [pl.BlockSpec(memory_space=pl.ANY)] + [here] * 4,
        out_specs=here,
        scratch_shapes=[
            pltpu.VMEM((groups, lanes, 2, each, tokens), jnp.bfloat16),
            pltpu.VMEM((groups, lanes, 2, each, tokens), jnp.bfloat16),
            pltpu.VMEM((2, lanes, each, tokens), jnp.bfloat16),
            pltpu.VMEM((2, lanes, each, tokens), jnp.bfloat16),
            pltpu.VMEM((lanes, each, tokens), jnp.float32),
            pltpu.VMEM((lanes, each, tokens), jnp.float32),
            pltpu.VMEM((groups, lanes, each, tokens), jnp.bfloat16),
            pltpu.VMEM((groups, lanes, each, tokens), jnp.bfloat16),
            pltpu.VMEM((groups, slabs, tokens, wide), jnp.bfloat16),
            pltpu.VMEM((groups, slabs, wide, columns), jnp.bfloat16),
            pltpu.VMEM((tokens, columns), jnp.float32),
            dma((groups, lanes)),
            dma((groups, lanes)),
            dma((groups, lanes)),
            dma((groups, lanes)),
            dma((groups, 3)),
            dma((groups, 3)),
            dma((slabs,)),
            dma((slabs,)),
            dma,
        ],
        compiler_params=pltpu.CompilerParams(
            collective_id=0, has_side_effects=True, vmem_limit_bytes=48 * 1024 * 1024
        ),
    )(
        inner_gate,
        values,
        outer_gate,
        filter_taps,
        skip_gain.reshape(1, channels),
        out_proj.reshape(groups, wide, out_proj.shape[1]),
        *tables,
    )


def on_device(inner_gate, *others):
    lanes = lax.axis_size("seq")
    tokens, channels = inner_gate.shape
    groups = channels // (16 * lanes)
    fits = (
        lax.axis_size("chan") == 4
        and groups >= 2
        and channels == groups * 16 * lanes
        and lanes % 8 == 0
        and tokens % BLK == 0
        and lanes & (lanes - 1) == 0
    )
    if fits:
        return kernel_on_device(lanes, groups, inner_gate, *others)
    return plain_on_device(inner_gate, *others)


def solution(mesh):
    return jax.shard_map(
        on_device,
        mesh=mesh,
        in_specs=(
            P("seq", "chan"),
            P("seq", "chan"),
            P("seq", "chan"),
            P("seq", "chan"),
            P("chan"),
            P("chan", None),
        ),
        out_specs=P("seq", "chan"),
        check_vma=False,
    )
```

profile of v0, /device:TPU:27, one launch (start us, length us, event | category | flops | bytes accessed | tf_op | source)
XLA Modules:
  0.0 60.2 jit_solution(14789207036061276373)
XLA Ops:
  0.0 0.0 copy-start
  0.0 1.2 %copy-done = f32[512,512]{1,0:T(8,128)S(1)} copy-done((f32[512,512]{1,0:T(8,128)S(1)}, f32[512,512]{1,0:T(8,128)}, u32[]{:S(2)}) %copy-start) | copy-done | bytes 1048600
  1.2 0.0 copy-start.1
  1.2 1.0 %copy-done.1 = bf16[512,512]{1,0:T(8,128)(2,1)S(1)} copy-done((bf16[512,512]{1,0:T(8,128)(2,1)S(1)}, bf16[512,512]{1,0:T(8,128)(2,1)}, u32[]{:S(2)}) %copy-start.1) | copy-done | bytes 524312
  2.3 0.0 copy-start.2
  2.3 1.0 %copy-done.2 = bf16[512,512]{1,0:T(8,128)(2,1)S(1)} copy-done((bf16[512,512]{1,0:T(8,128)(2,1)S(1)}, bf16[512,512]{1,0:T(8,128)(2,1)}, u32[]{:S(2)}) %copy-start.2) | copy-done | bytes 524312
  3.3 0.0 copy-start.3
  3.3 1.0 %copy-done.3 = bf16[512,512]{1,0:T(8,128)(2,1)S(1)} copy-done((bf16[512,512]{1,0:T(8,128)(2,1)S(1)}, bf16[512,512]{1,0:T(8,128)(2,1)}, u32[]{:S(2)}) %copy-start.3) | copy-done | bytes 524312
  4.4 0.0 copy-start.4
  4.4 1.0 %copy-done.4 = bf16[512,512]{1,0:T(8,128)(2,1)S(1)} copy-done((bf16[512,512]{1,0:T(8,128)(2,1)S(1)}, bf16[512,512]{1,0:T(8,128)(2,1)}, u32[]{:S(2)}) %copy-start.4) | copy-done | bytes 524312
  5.4 0.0 copy-start.5
  5.4 1.0 %copy-done.5 = bf16[512,512]{1,0:T(8,128)(2,1)S(1)} copy-done((bf16[512,512]{1,0:T(8,128)(2,1)S(1)}, bf16[512,512]{1,0:T(8,128)(2,1)}, u32[]{:S(2)}) %copy-start.5) | copy-done | bytes 524312
  6.4 0.0 copy-start.6
  6.4 0.7 %copy-done.6 = f32[8,512]{1,0:T(8,128)S(1)} copy-done((f32[8,512]{1,0:T(8,128)S(1)}, f32[8,512]{1,0:T(8,128)}, u32[]{:S(2)}) %copy-start.6) | copy-done | bytes 16408
  7.2 0.0 copy-start.7
  7.2 0.7 %copy-done.7 = f32[8,512]{1,0:T(8,128)S(1)} copy-done((f32[8,512]{1,0:T(8,128)S(1)}, f32[8,512]{1,0:T(8,128)}, u32[]{:S(2)}) %copy-start.7) | copy-done | bytes 16408
  7.9 0.0 copy-start.8
  7.9 0.7 %copy-done.8 = f32[512]{0:T(512)S(1)} copy-done((f32[512]{0:T(512)S(1)}, f32[512]{0:T(512)}, u32[]{:S(2)}) %copy-start.8) | copy-done | bytes 2072
  8.6 50.8 %shard_map.100 = bf16[512,512]{1,0:T(8,128)(2,1)S(1)} custom-call(bf16[512,512]{1,0:T(8,128)(2,1)S(1)} %copy-done.1, bf16[512,512]{1,0:T(8,128)(2,1)S(1)} %copy-done.2, bf16[512,512]{1,0:T(8,128)(2,1)S(1)} %copy-done.3, f32[512,512]{1,0:T(8,128)S(1)} %copy-done, f32[1,512]{1,0:T(1,128)S(1)} %bitcast.2, bf16[4,128,2048]{2,1,0:T(8,128)(2,1)} %bitcast.3, ...), custom_call_target="tpu_custom_call" | custom-call | tf_op jit(solution)/shard_map/pallas_call | solution.py:450
  59.4 0.8 %copy.12 = bf16[512,512]{1,0:T(8,128)(2,1)} copy(bf16[512,512]{1,0:T(8,128)(2,1)S(1)} %shard_map.100) | data formatting | bytes 1048576
Async XLA Ops:
  0.0 1.2 %copy-start = (f32[512,512]{1,0:T(8,128)S(1)}, f32[512,512]{1,0:T(8,128)}, u32[]{:S(2)}) copy-start(f32[512,512]{1,0:T(8,128)} %taps_ref.1) | copy-start | bytes 3145732
  1.2 1.0 %copy-start.1 = (bf16[512,512]{1,0:T(8,128)(2,1)S(1)}, bf16[512,512]{1,0:T(8,128)(2,1)}, u32[]{:S(2)}) copy-start(bf16[512,512]{1,0:T(8,128)(2,1)} %inner_ref.1) | copy-start | bytes 1572868
  2.3 1.0 %copy-start.2 = (bf16[512,512]{1,0:T(8,128)(2,1)S(1)}, bf16[512,512]{1,0:T(8,128)(2,1)}, u32[]{:S(2)}) copy-start(bf16[512,512]{1,0:T(8,128)(2,1)} %values_ref.1) | copy-start | bytes 1572868
  3.3 1.0 %copy-start.3 = (bf16[512,512]{1,0:T(8,128)(2,1)S(1)}, bf16[512,512]{1,0:T(8,128)(2,1)}, u32[]{:S(2)}) copy-start(bf16[512,512]{1,0:T(8,128)(2,1)} %outer_ref.1) | copy-start | bytes 1572868
  4.4 1.0 %copy-start.4 = (bf16[512,512]{1,0:T(8,128)(2,1)S(1)}, bf16[512,512]{1,0:T(8,128)(2,1)}, u32[]{:S(2)}) copy-start(bf16[512,512]{1,0:T(8,128)(2,1)} %constant.9.clone.sin_ref) | copy-start | bytes 1572868
  5.4 1.0 %copy-start.5 = (bf16[512,512]{1,0:T(8,128)(2,1)S(1)}, bf16[512,512]{1,0:T(8,128)(2,1)}, u32[]{:S(2)}) copy-start(bf16[512,512]{1,0:T(8,128)(2,1)} %constant.8.clone.cos_ref) | copy-start | bytes 1572868
  6.4 0.7 %copy-start.6 = (f32[8,512]{1,0:T(8,128)S(1)}, f32[8,512]{1,0:T(8,128)}, u32[]{:S(2)}) copy-start(f32[8,512]{1,0:T(8,128)} %constant.11.clone.turn_sin_ref) | copy-start | bytes 49156
  7.2 0.7 %copy-start.7 = (f32[8,512]{1,0:T(8,128)S(1)}, f32[8,512]{1,0:T(8,128)}, u32[]{:S(2)}) copy-start(f32[8,512]{1,0:T(8,128)} %constant.10.clone.turn_cos_ref) | copy-start | bytes 49156
  7.9 0.7 %copy-start.8 = (f32[512]{0:T(512)S(1)}, f32[512]{0:T(512)}, u32[]{:S(2)}) copy-start(f32[512]{0:T(512)} %param.14) | copy-start | bytes 6148
where the time goes:
time: 60.7 us; the launch traced here: 60.2 us
  Pallas kernels  50.8 us (84%)
  local copies, waits for them, and re-layouts  9.34 us (15%)
    pallas_call x1, Pallas kernels, kernel_on_device(): pl.pallas_call(functools.partial(mixer_kernel, lanes, groups), out_shape=...  50.8 us
    unnamed x19, local copies, waits for them, and re-layouts  9.34 us

commit v1 on v0

--- a/solution.py
+++ b/solution.py
@@ -188,17 +188,26 @@
 def mixer_kernel(
     lanes,
     groups,
+    inner_hbm,
+    values_hbm,
+    outer_hbm,
+    taps_hbm,
+    skip_hbm,
+    proj_ref,
+    cos_hbm,
+    sin_hbm,
+    turn_cos_hbm,
+    turn_sin_hbm,
+    out_ref,
     inner_ref,
     values_ref,
     outer_ref,
     taps_ref,
     skip_ref,
-    proj_ref,
     cos_ref,
     sin_ref,
     turn_cos_ref,
     turn_sin_ref,
-    out_ref,
     leave,
     arrive,
     sec_re,
@@ -219,6 +228,8 @@
     proj_send,
     proj_recv,
     proj_own,
+    piece_sem,
+    late_sem,
 ):
     me = lax.axis_index("seq")
     slab = lax.axis_index("chan")
@@ -231,6 +242,29 @@
     across = (slab + 2) % 4
     corner = (sibling + 2) % 4
 
+    def piece_copies(g):
+        cols = pl.ds(pl.multiple_of(g * wide, wide), wide)
+        pairs = ((inner_hbm, inner_ref), (values_hbm, values_ref), (taps_hbm, taps_ref))
+        return [
+            pltpu.make_async_copy(src.at[:, cols], dst.at[:, cols], piece_sem.at[g, i])
+            for i, (src, dst) in enumerate(pairs)
+        ]
+
+    def late_copies(first, last):
+        pairs = (
+            (turn_cos_hbm, turn_cos_ref),
+            (turn_sin_hbm, turn_sin_ref),
+            (cos_hbm, cos_ref),
+            (sin_hbm, sin_ref),
+            (outer_hbm, outer_ref),
+            (skip_hbm, skip_ref),
+        )
+        chosen = list(enumerate(pairs))[first:last]
+        return [pltpu.make_async_copy(src, dst, late_sem.at[i]) for i, (src, dst) in chosen]
+
+    for copy in piece_copies(0):
+        copy.start()
+
     barrier = pltpu.get_barrier_semaphore()
 
     @pl.loop(1, lanes)
@@ -244,7 +278,13 @@
             barrier, inc=1, device_id={"chan": (slab + step) % slabs}, device_id_type=MESH
         )
 
+    for g in range(1, groups):
+        for copy in piece_copies(g):
+            copy.start()
+
     def prepare(g):
+        for copy in piece_copies(g):
+            copy.wait()
         cols = pl.ds(pl.multiple_of(g * wide, wide), wide)
         mixed = inner_ref[:, cols].astype(jnp.float32) * values_ref[:, cols].astype(jnp.float32)
         mixed = mixed.T.astype(jnp.bfloat16)
@@ -310,6 +350,8 @@
     def _(step):
         in_copy(0, step, me).start()
 
+    for copy in late_copies(0, 6):
+        copy.start()
     own_proj.start()
     for step in range(1, slabs):
         proj_copy(step, slab).start()
@@ -321,6 +363,9 @@
         @pl.loop(1, lanes)
         def _(step):
             in_copy(g, step, me).start()
+
+    for copy in late_copies(0, 4):
+        copy.wait()
 
     def dot(left, right):
         return jnp.dot(left, right, preferred_element_type=jnp.float32)
@@ -380,6 +425,9 @@
     def forward(g):
         side_copy(g, 1, across, across).wait_recv()
         side_copy(g, 2, across, sibling).start()
+
+    for copy in late_copies(4, 6):
+        copy.wait()
 
     for g in range(groups):
 
@@ -450,9 +498,18 @@
     return pl.pallas_call(
         functools.partial(mixer_kernel, lanes, groups),
         out_shape=jax.ShapeDtypeStruct((tokens, columns), jnp.bfloat16),
-        in_specs=[here] * 5 + [pl.BlockSpec(memory_space=pl.ANY)] + [here] * 4,
+        in_specs=[pl.BlockSpec(memory_space=pltpu.HBM)] * 10,
         out_specs=here,
         scratch_shapes=[
+            pltpu.VMEM((tokens, channels), jnp.bfloat16),
+            pltpu.VMEM((tokens, channels), jnp.bfloat16),
+            pltpu.VMEM((tokens, channels), jnp.bfloat16),
+            pltpu.VMEM((tokens, channels), jnp.float32),
+            pltpu.VMEM((1, channels), jnp.float32),
+            pltpu.VMEM((tokens, tokens), jnp.bfloat16),
+            pltpu.VMEM((tokens, tokens), jnp.bfloat16),
+            pltpu.VMEM((lanes, tokens), jnp.float32),
+            pltpu.VMEM((lanes, tokens), jnp.float32),
             pltpu.VMEM((groups, lanes, 2, each, tokens), jnp.bfloat16),
             pltpu.VMEM((groups, lanes, 2, each, tokens), jnp.bfloat16),
             pltpu.VMEM((2, lanes, each, tokens), jnp.bfloat16),
@@ -473,9 +530,11 @@
             dma((slabs,)),
             dma((slabs,)),
             dma,
+            dma((groups, 3)),
+            dma((6,)),
         ],
         compiler_params=pltpu.CompilerParams(
-            collective_id=0, has_side_effects=True, vmem_limit_bytes=48 * 1024 * 1024
+            collective_id=0, has_side_effects=True, vmem_limit_bytes=63 * 1024 * 1024
         ),
     )(
         inner_gate,

time: 60.7 us -> 53.9 us (0.89)
  local copies, waits for them, and re-layouts: 9.34 us -> 1.87 us
  Pallas kernels: 50.8 us -> 51.8 us
    unnamed x19 -> x1, local copies, waits for them, and re-layouts: 9.34 us -> 1.87 us
    pallas_call x1, Pallas kernels: 50.8 us -> 51.8 us  [kernel_on_device(): pl.pallas_call(functools.partial(mixer_kernel, lanes, groups), out_shape=...]
where the time goes in v1:
time: 53.9 us; the launch traced here: 53.7 us
  Pallas kernels  51.8 us (96%)
  local copies, waits for them, and re-layouts  1.87 us (3%)
    pallas_call x1, Pallas kernels, kernel_on_device(): pl.pallas_call(functools.partial(mixer_kernel, lanes, groups), out_shape=...  51.8 us
    unnamed x1, local copies, waits for them, and re-layouts  1.87 us

profile of v1, /device:TPU:27, one launch (start us, length us, event | category | flops | bytes accessed | tf_op | source)
XLA Modules:
  0.0 53.7 jit_solution(10371218896121616059)
XLA Ops:
  0.0 51.8 %shard_map.100 = bf16[512,512]{1,0:T(8,128)(2,1)} custom-call(bf16[512,512]{1,0:T(8,128)(2,1)} %inner_hbm.1, bf16[512,512]{1,0:T(8,128)(2,1)} %values_hbm.1, bf16[512,512]{1,0:T(8,128)(2,1)} %outer_hbm.1, f32[512,512]{1,0:T(8,128)} %taps_hbm.1, f32[1,512]{1,0:T(1,128)} %bitcast.3, bf16[4,128,2048]{2,1,0:T(8,128)(2,1)} %bitcast.2, ...), custom_call_target="tpu_custom_call" | custom-call | tf_op jit(solution)/shard_map/pallas_call | solution.py:498
  51.8 1.9 %copy.12 = bf16[512,512]{1,0:T(8,128)(2,1)} copy(bf16[512,512]{1,0:T(8,128)(2,1)} %shard_map.100) | data formatting | bytes 1048576

commit v2 on v1

--- a/solution.py
+++ b/solution.py
@@ -282,6 +282,13 @@
         for copy in piece_copies(g):
             copy.start()
 
+    def spread(send):
+        half = lanes // 2
+
+        @pl.loop(0, lanes - 1)
+        def _(i):
+            send(half + (1 - 2 * (i % 2)) * ((i + 1) // 2))
+
     def prepare(g):
         for copy in piece_copies(g):
             copy.wait()
@@ -346,9 +353,7 @@
         proj_own,
     )
 
-    @pl.loop(1, lanes)
-    def _(step):
-        in_copy(0, step, me).start()
+    spread(lambda step: in_copy(0, step, me).start())
 
     for copy in late_copies(0, 6):
         copy.start()
@@ -360,9 +365,7 @@
     def _(g):
         prepare(g)
 
-        @pl.loop(1, lanes)
-        def _(step):
-            in_copy(g, step, me).start()
+        spread(lambda step: in_copy(g, step, me).start())
 
     for copy in late_copies(0, 4):
         copy.wait()
@@ -416,9 +419,7 @@
                     jnp.bfloat16
                 )
 
-        @pl.loop(1, lanes)
-        def _(step):
-            conv_copy(g, step, me).start()
+        spread(lambda step: conv_copy(g, step, me).start())
 
         conv_arrive[g, me] = conv_leave[g, me]
 
@@ -426,32 +427,7 @@
         side_copy(g, 1, across, across).wait_recv()
         side_copy(g, 2, across, sibling).start()
 
-    for copy in late_copies(4, 6):
-        copy.wait()
-
-    for g in range(groups):
-
-        @pl.loop(1, lanes)
-        def _(step):
-            conv_copy(g, step, (me + lanes - step) % lanes).wait_recv()
-
-        cols = slice(g * wide, (g + 1) * wide)
-        conv = conv_arrive[g].astype(jnp.float32).reshape(wide, tokens).T
-        gated = outer_ref[:, cols].astype(jnp.float32) * (
-            conv + skip_ref[:, cols] * values_ref[:, cols].astype(jnp.float32)
-        )
-        gathered[g, slab] = gated.astype(jnp.bfloat16)
-        side_copy(g, 1, slab, across).start()
-        side_copy(g, 0, slab, sibling).start()
-        if g > 0:
-            forward(g - 1)
-    forward(groups - 1)
-
-    own_proj.wait()
-    for step in range(1, slabs):
-        proj_copy(step, (slab + slabs - step) % slabs).wait_recv()
-
-    for g in range(groups):
+    def project(g):
         side_copy(g, 0, sibling, sibling).wait_recv()
         side_copy(g, 2, corner, sibling).wait_recv()
         left = jnp.concatenate([gathered[g, j] for j in range(slabs)], axis=1)
@@ -462,6 +438,34 @@
             total[...] += part
         else:
             out_ref[...] = (total[...] + part).astype(out_ref.dtype)
+
+    for copy in late_copies(4, 6):
+        copy.wait()
+    own_proj.wait()
+    for step in range(1, slabs):
+        proj_copy(step, (slab + slabs - step) % slabs).wait_recv()
+
+    for g in range(groups):
+
+        @pl.loop(1, lanes)
+        def _(step):
+            conv_copy(g, step, (me + lanes - step) % lanes).wait_recv()
+
+        cols = slice(g * wide, (g + 1) * wide)
+        conv = conv_arrive[g].astype(jnp.float32).reshape(wide, tokens).T
+        gated = outer_ref[:, cols].astype(jnp.float32) * (
+            conv + skip_ref[:, cols] * values_ref[:, cols].astype(jnp.float32)
+        )
+        gathered[g, slab] = gated.astype(jnp.bfloat16)
+        side_copy(g, 1, slab, across).start()
+        side_copy(g, 0, slab, sibling).start()
+        if g > 0:
+            forward(g - 1)
+        if g > 1:
+            project(g - 2)
+    project(groups - 2)
+    forward(groups - 1)
+    project(groups - 1)
 
     @pl.loop(0, groups)
     def _(g):

time: 53.9 us -> 53.2 us (0.987)
  the two profiles are of different devices: /device:TPU:27 before, /device:TPU:21 now
where the time goes in v2:
time: 53.2 us; the launch traced here: 53 us
  Pallas kernels  51.2 us (96%)
  local copies, waits for them, and re-layouts  1.87 us (4%)
    pallas_call x1, Pallas kernels, kernel_on_device(): pl.pallas_call(functools.partial(mixer_kernel, lanes, groups), out_shape=...  51.2 us
    unnamed x1, local copies, waits for them, and re-layouts  1.87 us

profile of v2, /device:TPU:21, one launch (start us, length us, event | category | flops | bytes accessed | tf_op | source)
XLA Modules:
  0.0 53.0 jit_solution(17508538038420108884)
XLA Ops:
  0.0 51.2 %shard_map.100 = bf16[512,512]{1,0:T(8,128)(2,1)} custom-call(bf16[512,512]{1,0:T(8,128)(2,1)} %inner_hbm.1, bf16[512,512]{1,0:T(8,128)(2,1)} %values_hbm.1, bf16[512,512]{1,0:T(8,128)(2,1)} %outer_hbm.1, f32[512,512]{1,0:T(8,128)} %taps_hbm.1, f32[1,512]{1,0:T(1,128)} %bitcast.3, bf16[4,128,2048]{2,1,0:T(8,128)(2,1)} %bitcast.2, ...), custom_call_target="tpu_custom_call" | custom-call | tf_op jit(solution)/shard_map/pallas_call | solution.py:502
  51.2 1.9 %copy.12 = bf16[512,512]{1,0:T(8,128)(2,1)} copy(bf16[512,512]{1,0:T(8,128)(2,1)} %shard_map.100) | data formatting | bytes 1048576
